TPU v7x, 128 devices: a whole 4x4x4 slice. The times are simulated.
128 devices in a mesh: seq: 16 (over x, z), exp: 8 (over y, core).
Axes of the slice: x: 4, y: 4, z: 4, core: 2. Of those that a mesh axis runs over, the one named last changes fastest.
Arguments:
- stream: bfloat16 [8, 2048, 2048], P('exp', 'seq'), may hold values from -6 to 6
- stream_tangent: bfloat16 [8, 2048, 2048], P('exp', 'seq'), may hold values from -6 to 6
- query_rows: bfloat16 [8, 2048, 2048], P('exp', 'seq'), may hold values from -6 to 6
- key_rows: bfloat16 [8, 2048, 2048], P('exp', 'seq'), may hold values from -6 to 6
- value_rows: bfloat16 [8, 2048, 2048], P('exp', 'seq'), may hold values from -6 to 6
- query_tangent: bfloat16 [8, 2048, 2048], P('exp', 'seq'), may hold values from -6 to 6
- key_tangent: bfloat16 [8, 2048, 2048], P('exp', 'seq'), may hold values from -6 to 6
- value_tangent: bfloat16 [8, 2048, 2048], P('exp', 'seq'), may hold values from -6 to 6
- out_proj: bfloat16 [2048, 2048], P('seq'), may hold values from -0.375 to 0.375
- norm_gain: bfloat16 [2048], replicated, may hold values from 0.099609375 to 1.8984375
- gate_weight: bfloat16 [8, 2048, 1408], P('exp'), may hold values from -0.125 to 0.125
- up_weight: bfloat16 [8, 2048, 1408], P('exp'), may hold values from -0.125 to 0.125
- down_weight: bfloat16 [8, 1408, 2048], P('exp'), may hold values from -0.15625 to 0.15625
- route_ids: int32 [8, 2048, 2], P('exp', 'seq'), may hold values from 0 to 7, all different within a row; in each aligned block of 128 rows (0 to 127, 128 to 255, ..., all dimensions but the last counted through in order) at most 64 rows name the same one
- route_weights: bfloat16 [8, 2048, 2], P('exp', 'seq'), may hold values from 0.25 to 1
Outputs:
- layer_out: bfloat16 [8, 2048, 2048], P('exp', 'seq')
- layer_tangent: bfloat16 [8, 2048, 2048], P('exp', 'seq')
Inputs may be any that keep to these rules, and one draw needn't show every extreme that they name: `route_ids`: A token's 2 experts differ. Among the 128 tokens of one device (aligned blocks of positions of one sequence), no expert is named more than 64 times, a bound that some block reaches.
All inputs are finite; a program needn't handle non-finite values.
Results may differ from a plain program's by a relative error of at most 0.019.
Values may be sent and summed in bfloat16 or wider, within the bound.
No kernel may reach another device: no remote copies, remote signals or barrier semaphores. Data moves between devices by JAX's collectives and lax.ppermute only.
A program may use at most 192 MiB of HBM per device.

v0:
```python
import functools
import math

import jax
import jax.numpy as jnp
from jax import lax
from jax.experimental import pallas as pl
from jax.experimental.pallas import tpu as pltpu
from jax.sharding import PartitionSpec as P

HEAD_DIM = 128
BF16 = jnp.bfloat16
F32 = jnp.float32
MIB = 2**20


def dot(a, b):
    return jnp.dot(a, b, preferred_element_type=F32)


def pack_kernel(*refs):
    ins, out = refs[:-1], refs[-1]
    heads = out.shape[0]
    for h in range(heads):
        for a, ref in enumerate(ins):
            out[h, a] = ref[:, h * HEAD_DIM : (h + 1) * HEAD_DIM]


def pack(arrays):
    rows, width = arrays[0].shape
    heads = width // HEAD_DIM
    step = 4
    return pl.pallas_call(
        pack_kernel,
        grid=(heads // step,),
        out_shape=jax.ShapeDtypeStruct((heads, len(arrays), rows, HEAD_DIM), BF16),
        in_specs=[pl.BlockSpec((rows, step * HEAD_DIM), lambda i: (0, i))] * len(arrays),
        out_specs=pl.BlockSpec((step, len(arrays), rows, HEAD_DIM), lambda i: (i, 0, 0, 0)),
        cost_estimate=pl.CostEstimate(
            flops=0, bytes_accessed=4 * len(arrays) * rows * width, transcendentals=0
        ),
        name="pack_heads",
    )(*arrays)


def attend_kernel(blocks, r_ref, o_ref, kt, vv):
    sources, _, rows, _ = r_ref.shape
    i = pl.program_id(0)

    @pl.when(i == 0)
    def _():
        for s in range(sources):
            at = slice(s * rows, (s + 1) * rows)
            kt[:HEAD_DIM, at] = r_ref[s, 1].T
            kt[HEAD_DIM:, at] = r_ref[s, 4].T
            vv[at, :HEAD_DIM] = r_ref[s, 2]
            vv[at, HEAD_DIM:] = r_ref[s, 5]

    scale = 1.0 / math.sqrt(HEAD_DIM)
    q = r_ref[pl.ds(i * blocks, blocks), 0].reshape(blocks * rows, HEAD_DIM)
    dq = r_ref[pl.ds(i * blocks, blocks), 3].reshape(blocks * rows, HEAD_DIM)
    s = dot(q, kt[:HEAD_DIM])
    ds = dot(jnp.concatenate([dq, q], axis=1), kt[...])
    m = jnp.max(s, axis=-1, keepdims=True)
    e = jnp.exp2((s - m) * (scale * math.log2(math.e)))
    total = jnp.sum(e, axis=-1, keepdims=True)
    w = e * ds
    row_sum = jnp.sum(w, axis=-1, keepdims=True)
    both = dot(e.astype(BF16), vv[...])
    wv = dot(w.astype(BF16), vv[:, :HEAD_DIM])
    inv = 1.0 / total
    att = both[:, :HEAD_DIM] * inv
    tan = (wv * scale + both[:, HEAD_DIM:]) * inv - (row_sum * (inv * scale)) * att
    o_ref[:, 0] = att.astype(BF16).reshape(blocks, rows, HEAD_DIM)
    o_ref[:, 1] = tan.astype(BF16).reshape(blocks, rows, HEAD_DIM)


def attend(received, blocks=2):
    sources, _, rows, _ = received.shape
    seq_len = sources * rows
    return pl.pallas_call(
        functools.partial(attend_kernel, blocks),
        grid=(sources // blocks,),
        out_shape=jax.ShapeDtypeStruct((sources, 2, rows, HEAD_DIM), BF16),
        in_specs=[pl.BlockSpec(received.shape, lambda i: (0, 0, 0, 0))],
        out_specs=pl.BlockSpec((blocks, 2, rows, HEAD_DIM), lambda i: (i, 0, 0, 0)),
        scratch_shapes=[
            pltpu.VMEM((2 * HEAD_DIM, seq_len), BF16),
            pltpu.VMEM((seq_len, 2 * HEAD_DIM), BF16),
        ],
        compiler_params=pltpu.CompilerParams(vmem_limit_bytes=48 * MIB),
        cost_estimate=pl.CostEstimate(
            flops=16 * seq_len * seq_len * HEAD_DIM,
            bytes_accessed=16 * seq_len * HEAD_DIM,
            transcendentals=seq_len * seq_len,
        ),
        name="attend_head",
    )(received)


def project_kernel(a_ref, w_ref, s_ref, ds_ref, g_ref, h_ref, n_ref, x, acc):
    heads, _, rows, _ = a_ref.shape
    tile = w_ref.shape[2]
    i = pl.program_id(0)

    @pl.when(i == 0)
    def _():
        for h in range(heads):
            at = slice(h * HEAD_DIM, (h + 1) * HEAD_DIM)
            x[:rows, at] = a_ref[h, 0]
            x[rows:, at] = a_ref[h, 1]

    out = dot(x[...], w_ref[0])
    at = pl.ds(pl.multiple_of(i * tile, tile), tile)
    acc[:rows, at] = out[:rows] + s_ref[:, at].astype(F32)
    acc[rows:, at] = out[rows:] + ds_ref[:, at].astype(F32)

    @pl.when(i == pl.num_programs(0) - 1)
    def _():
        hid = acc[:rows, :]
        tan = acc[rows:, :]
        gain = g_ref[...].astype(F32)
        inverse = lax.rsqrt(jnp.mean(hid * hid, axis=-1, keepdims=True) + 1e-06)
        cross = jnp.mean(hid * tan, axis=-1, keepdims=True)
        width = hid.shape[1]
        h_ref[:, :width] = hid
        h_ref[:, width:] = tan
        n_ref[:, :width] = (hid * inverse * gain).astype(BF16)
        n_ref[:, width:] = (
            gain * (tan * inverse - hid * (inverse * inverse * inverse) * cross)
        ).astype(BF16)


def project(attended, weights, stream, stream_tangent, gain):
    tiles, width, tile = weights.shape
    rows = stream.shape[0]
    full = lambda shape: pl.BlockSpec(shape, lambda i: (0,) * len(shape))
    return pl.pallas_call(
        project_kernel,
        grid=(tiles,),
        out_shape=(
            jax.ShapeDtypeStruct((rows, 2 * width), F32),
            jax.ShapeDtypeStruct((rows, 2 * width), BF16),
        ),
        in_specs=[
            full(attended.shape),
            pl.BlockSpec((1, width, tile), lambda i: (i, 0, 0)),
            full(stream.shape),
            full(stream.shape),
            full((1, width)),
        ],
        out_specs=(full((rows, 2 * width)), full((rows, 2 * width))),
        scratch_shapes=[
            pltpu.VMEM((2 * rows, width), BF16),
            pltpu.VMEM((2 * rows, width), F32),
        ],
        compiler_params=pltpu.CompilerParams(vmem_limit_bytes=48 * MIB),
        cost_estimate=pl.CostEstimate(
            flops=4 * rows * width * width, bytes_accessed=3 * width * width, transcendentals=0
        ),
        name="project_norm",
    )(attended, weights, stream, stream_tangent, gain)


def expert_kernel(up_steps, x_ref, g_ref, u_ref, d_ref, o_ref, hid):
    rows = x_ref.shape[0]
    width = x_ref.shape[1] // 2
    tile = g_ref.shape[1]
    i = pl.program_id(0)
    block = 256

    @pl.when(i < up_steps)
    def _():
        at = pl.ds(pl.multiple_of(i * tile, tile), tile)
        weights = jnp.concatenate([g_ref[...], u_ref[...]], axis=1)

        def step(j, carry):
            r = pl.ds(pl.multiple_of(j * block, block), block)
            primal = dot(x_ref[r, :width], weights)
            tangent = dot(x_ref[r, width:], weights)
            gate, up = primal[:, :tile], primal[:, tile:]
            dgate, dup = tangent[:, :tile], tangent[:, tile:]
            sig = jax.nn.sigmoid(gate)
            act = gate * sig
            slope = sig * (1.0 + gate * (1.0 - sig))
            hid[0, r, at] = (act * up).astype(BF16)
            hid[1, r, at] = (slope * dgate * up + act * dup).astype(BF16)
            return carry

        lax.fori_loop(0, rows // block, step, 0, unroll=True)

    @pl.when(i >= up_steps)
    def _():
        def step(j, carry):
            r = pl.ds(pl.multiple_of(j * block, block), block)
            o_ref[0, r] = dot(hid[0, r], d_ref[...]).astype(BF16)
            o_ref[1, r] = dot(hid[1, r], d_ref[...]).astype(BF16)
            return carry

        lax.fori_loop(0, rows // block, step, 0, unroll=True)


def expert(x, gate, up, down):
    rows, both = x.shape
    width, ff = gate.shape
    tile = 128
    up_steps = ff // tile
    cols = 256
    down_steps = width // cols
    return pl.pallas_call(
        functools.partial(expert_kernel, up_steps),
        grid=(up_steps + down_steps,),
        out_shape=jax.ShapeDtypeStruct((2, rows, width), BF16),
        in_specs=[
            pl.BlockSpec((rows, both), lambda i: (0, 0)),
            pl.BlockSpec((width, tile), lambda i: (0, jnp.minimum(i, up_steps - 1))),
            pl.BlockSpec((width, tile), lambda i: (0, jnp.minimum(i, up_steps - 1))),
            pl.BlockSpec((ff, cols), lambda i: (0, jnp.maximum(i - up_steps, 0))),
        ],
        out_specs=pl.BlockSpec((2, rows, cols), lambda i: (0, 0, jnp.maximum(i - up_steps, 0))),
        scratch_shapes=[pltpu.VMEM((2, rows, ff), BF16)],
        compiler_params=pltpu.CompilerParams(vmem_limit_bytes=48 * MIB),
        cost_estimate=pl.CostEstimate(
            flops=12 * rows * width * ff, bytes_accessed=6 * width * ff + 8 * rows * both,
            transcendentals=rows * ff,
        ),
        name="expert_rows",
    )(x, gate, up, down)


def shards(
    stream,
    stream_tangent,
    query_rows,
    key_rows,
    value_rows,
    query_tangent,
    key_tangent,
    value_tangent,
    out_proj,
    norm_gain,
    gate_weight,
    up_weight,
    down_weight,
    route_ids,
    route_weights,
):
    owner_count = lax.axis_size("exp")
    tok_dev, width = stream.shape[1:]
    own = lax.axis_index("exp")

    cols = width // owner_count
    own_cols = lax.dynamic_slice_in_dim(out_proj, own * cols, cols, axis=1)
    own_cols = lax.all_gather(own_cols, "seq", axis=0, tiled=True)
    weights = lax.all_gather(own_cols, "exp", axis=0, tiled=False)

    sent = pack(
        [
            query_rows[0],
            key_rows[0],
            value_rows[0],
            query_tangent[0],
            key_tangent[0],
            value_tangent[0],
        ]
    )
    received = lax.all_to_all(sent, "seq", split_axis=0, concat_axis=0, tiled=True)
    attended = attend(received)
    returned = lax.all_to_all(attended, "seq", split_axis=0, concat_axis=0, tiled=True)
    hidden, normed = project(
        returned, weights, stream[0], stream_tangent[0], norm_gain.reshape(1, -1)
    )

    topk_count = route_ids.shape[2]
    experts_total = owner_count * gate_weight.shape[0]
    capacity = 2 * tok_dev * topk_count // experts_total
    flat_ids = route_ids.reshape(-1)
    onehot = (flat_ids[:, None] == jnp.arange(experts_total, dtype=jnp.int32)[None, :]).astype(
        jnp.int32
    )
    rank_in = jnp.sum((jnp.cumsum(onehot, axis=0) - onehot) * onehot, axis=1)
    slot_ids = (flat_ids * capacity + rank_in).reshape(tok_dev, topk_count)
    slot_index = jnp.arange(experts_total * capacity, dtype=jnp.int32)
    slot_hits = slot_ids[None, :, :] == slot_index[:, None, None]
    dispatch_matrix = jnp.sum(slot_hits.astype(jnp.int32), axis=-1).astype(BF16)
    combine_matrix = jnp.sum(
        jnp.where(slot_hits, route_weights[0][None, :, :], 0.0).astype(F32), axis=-1
    ).astype(BF16)

    send_rows = dot(dispatch_matrix, normed).astype(BF16)
    send_rows = send_rows.reshape(owner_count, capacity, 2 * width)
    arrived = lax.all_to_all(send_rows, "exp", split_axis=0, concat_axis=0, tiled=True)
    processed = expert(
        arrived.reshape(owner_count * capacity, 2 * width),
        gate_weight[0],
        up_weight[0],
        down_weight[0],
    )
    processed = processed.reshape(2, owner_count, capacity, width)
    results = lax.all_to_all(processed, "exp", split_axis=1, concat_axis=1, tiled=True)
    results = results.reshape(2, experts_total * capacity, width)
    mixed = jnp.einsum("st,psd->ptd", combine_matrix, results, preferred_element_type=F32)
    layer_out = (hidden[:, :width] + mixed[0]).astype(BF16)[None]
    layer_tangent = (hidden[:, width:] + mixed[1]).astype(BF16)[None]
    return (layer_out, layer_tangent)


def solution(mesh):
    rows = P("exp", "seq", None)
    in_specs = (rows,) * 8 + (
        P("seq", None),
        P(),
        P("exp", None, None),
        P("exp", None, None),
        P("exp", None, None),
        rows,
        rows,
    )
    return jax.shard_map(
        shards, mesh=mesh, in_specs=in_specs, out_specs=(rows, rows), check_vma=False
    )
```

profile of v0, /device:TPU:1, one launch (start us, length us, event | category | flops | bytes accessed | tf_op | source)
XLA Modules:
  0.0 298.9 jit_solution(2091935437265108328)
XLA Ops:
  7.2 1.0 copy-done
  8.2 0.6 constant_dynamic-slice_fusion
  8.9 46.4 %all-gather.4.cloned.1.call-done = bf16[2048,256]{1,0:T(8,128)(2,1)} async-done(((bf16[128,256]{1,0:T(8,128)(2,1)}), bf16[2048,256]{1,0:T(8,128)(2,1)}) %all-gather.4.cloned.1.call-update) | async-done | bytes 1048592 | tf_op jit(solution)/shard_map/all_gather | solution.py:254
  55.4 4.5 %pack_heads.1 = bf16[16,6,128,128]{3,2,1,0:T(8,128)(2,1)} custom-call(bf16[128,2048]{1,0:T(8,128)(2,1)} %bitcast.61, bf16[128,2048]{1,0:T(8,128)(2,1)} %bitcast.62, bf16[128,2048]{1,0:T(8,128)(2,1)} %bitcast.63, bf16[128,2048]{1,0:T(8,128)(2,1)} %bitcast.64, bf16[128,2048]{1,0:T(8,128)(2,1)} %bitcast.65, bf16[128,2048]{1,0:T(8,128)(2,1)} %bitcast.66), custom_call_target="tpu_custom_call" | custom-call | bytes 6291456 | tf_op jit(solution)/shard_map/pack_heads/pallas_call | solution.py:33
  59.9 41.6 %all_to_all.20.r_ref = bf16[16,6,128,128]{3,2,1,0:T(8,128)(2,1)S(1)} all-to-all(bf16[16,6,128,128]{3,2,1,0:T(8,128)(2,1)} %pack_heads.1), channel_id=1, replica_groups=mesh['seq'=16,'exp'=8] {'seq'}, dimensions={0} | all-to-all | bytes 6291456 | tf_op jit(solution)/shard_map/all_to_all | solution.py:267
  101.5 14.0 %attend_head.1 = bf16[16,2,128,128]{3,2,1,0:T(8,128)(2,1)} custom-call(bf16[16,6,128,128]{3,2,1,0:T(8,128)(2,1)S(1)} %all_to_all.20.r_ref), custom_call_target="tpu_custom_call" | custom-call | flops 8589934592 | bytes 4194304 | tf_op jit(solution)/shard_map/attend_head/pallas_call | solution.py:81
  115.4 5.5 %all-to-all-start.1 = ((bf16[16,2,128,128]{3,2,1,0:T(8,128)(2,1)}), bf16[16,2,128,128]{3,2,1,0:T(8,128)(2,1)S(1)}, u32[]{:S(2)}, u32[]{:S(2)}) async-start(bf16[16,2,128,128]{3,2,1,0:T(8,128)(2,1)} %attend_head.1), calls=%async_computation.1 | async-start | bytes 2097152 | tf_op jit(solution)/shard_map/all_to_all | solution.py:269
  121.2 0.1 eq.40
  121.4 0.6 reduce-window.6
  122.0 0.2 slice_reduce_fusion
  122.3 0.1 reduce_sum.33
  122.6 13.0 %all-to-all-done.1.a_ref = bf16[16,2,128,128]{3,2,1,0:T(8,128)(2,1)S(1)} async-done(((bf16[16,2,128,128]{3,2,1,0:T(8,128)(2,1)}), bf16[16,2,128,128]{3,2,1,0:T(8,128)(2,1)S(1)}, u32[]{:S(2)}, u32[]{:S(2)}) %all-to-all-start.1) | async-done | bytes 1048608 | tf_op jit(solution)/shard_map/all_to_all | solution.py:269
  135.6 1.0 copy-done.2
  136.7 1.0 copy-done.3
  137.7 8.6 %project_norm.1 = (f32[128,4096]{1,0:T(8,128)S(1)}, bf16[128,4096]{1,0:T(8,128)(2,1)S(1)}) custom-call(bf16[16,2,128,128]{3,2,1,0:T(8,128)(2,1)S(1)} %all-to-all-done.1.a_ref, bf16[8,2048,256]{2,1,0:T(8,128)(2,1)} %bitcast.59, bf16[128,2048]{1,0:T(8,128)(2,1)S(1)} %bitcast.55, bf16[128,2048]{1,0:T(8,128)(2,1)S(1)} %bitcast.56, bf16[1,2048]{1,0:T(2,128)(2,1)S(1)} %reshape.38.g_ref), custom_call_target="tpu_custom_call" | custom-call | flops 2147483648 | bytes 12582912 | tf_op jit(solution)/shard_map/project_norm/pallas_call | solution.py:138
  146.3 1.2 convolution_convert_fusion
  147.6 56.8 %all_to_all.21 = bf16[8,64,4096]{2,1,0:T(8,128)(2,1)} all-to-all(bf16[8,64,4096]{2,1,0:T(8,128)(2,1)S(1)} %bitcast.57), channel_id=1, replica_groups=mesh['seq'=16,'exp'=8] {'exp'}, dimensions={0} | all-to-all | bytes 8388608 | tf_op jit(solution)/shard_map/all_to_all | solution.py:292
  204.4 26.1 %expert_rows.1 = bf16[2,512,2048]{2,1,0:T(8,128)(2,1)S(1)} custom-call(bf16[512,4096]{1,0:T(8,128)(2,1)} %bitcast.60, bf16[2048,1408]{1,0:T(8,128)(2,1)} %bitcast.68, bf16[2048,1408]{1,0:T(8,128)(2,1)} %bitcast.69, bf16[1408,2048]{1,0:T(8,128)(2,1)} %bitcast.70), custom_call_target="tpu_custom_call" | custom-call | flops 17716740096 | bytes 34078720 | tf_op jit(solution)/shard_map/expert_rows/pallas_call | solution.py:210
  230.5 2.5 copy.49
  233.0 5.6 %all-to-all-start.3 = ((bf16[2,8,64,2048]{3,2,0,1:T(8,128)(2,1)}), bf16[2,8,64,2048]{3,2,0,1:T(8,128)(2,1)}, u32[]{:S(2)}, u32[]{:S(2)}) async-start(bf16[2,8,64,2048]{3,2,0,1:T(8,128)(2,1)} %copy.49), calls=%async_computation.3 | async-start | bytes 8388608 | tf_op jit(solution)/shard_map/all_to_all | solution.py:300
  238.7 48.9 %all-to-all-done.3 = bf16[2,8,64,2048]{3,2,0,1:T(8,128)(2,1)} async-done(((bf16[2,8,64,2048]{3,2,0,1:T(8,128)(2,1)}), bf16[2,8,64,2048]{3,2,0,1:T(8,128)(2,1)}, u32[]{:S(2)}, u32[]{:S(2)}) %all-to-all-start.3) | async-done | bytes 4194336 | tf_op jit(solution)/shard_map/all_to_all | solution.py:300
  287.6 2.5 copy.50
  290.1 0.8 convolution_bitcast_fusion
  290.8 1.2 fusion.5
  (27 shorter events, 0.8 us)
Async XLA Ops:
  7.2 1.1 copy-start
  7.2 48.2 %all-gather.4.cloned.1.call-start = ((), (), s32[]{:S(2)}) async-start(), calls=%async_computation.4 | async-start | bytes 1114112 | tf_op jit(solution)/shard_map/all_gather | solution.py:254
  8.9 126.8 %all-gather.6.cloned.1.call-start = ((), (), s32[]{:S(2)}) async-start(), calls=%async_computation.5 | async-start | bytes 9437184 | tf_op jit(solution)/shard_map/all_gather | solution.py:255
  101.4 19.5 %copy-start.4 = (s32[1,128,2]{1,2,0:T(2,128)S(1)}, s32[1,128,2]{1,2,0:T(2,128)}, u32[]{:S(2)}) copy-start(s32[1,128,2]{1,2,0:T(2,128)} %param.28) | copy-start | bytes 3076
  101.5 19.9 %copy-start.5 = (bf16[2048]{0:T(1024)(128)(2,1)S(1)}, bf16[2048]{0:T(1024)(128)(2,1)}, u32[]{:S(2)}) copy-start(bf16[2048]{0:T(1024)(128)(2,1)} %param.24) | copy-start | bytes 12292
  115.4 20.2 %all-to-all-start.1 = ((bf16[16,2,128,128]{3,2,1,0:T(8,128)(2,1)}), bf16[16,2,128,128]{3,2,1,0:T(8,128)(2,1)S(1)}, u32[]{:S(2)}, u32[]{:S(2)}) async-start(bf16[16,2,128,128]{3,2,1,0:T(8,128)(2,1)} %attend_head.1), calls=%async_computation.1 | async-start | bytes 2097152 | tf_op jit(solution)/shard_map/all_to_all | solution.py:269
  135.6 1.0 copy-start.2
  136.7 1.0 copy-start.3
  233.0 5.6 %copy-start.6 = (bf16[1,128,2]{1,2,0:T(2,128)(2,1)S(1)}, bf16[1,128,2]{1,2,0:T(2,128)(2,1)}, u32[]{:S(2)}) copy-start(bf16[1,128,2]{1,2,0:T(2,128)(2,1)} %param.29) | copy-start | bytes 1540
  233.0 54.5 %all-to-all-start.3 = ((bf16[2,8,64,2048]{3,2,0,1:T(8,128)(2,1)}), bf16[2,8,64,2048]{3,2,0,1:T(8,128)(2,1)}, u32[]{:S(2)}, u32[]{:S(2)}) async-start(bf16[2,8,64,2048]{3,2,0,1:T(8,128)(2,1)} %copy.49), calls=%async_computation.3 | async-start | bytes 8388608 | tf_op jit(solution)/shard_map/all_to_all | solution.py:300
  290.1 2.0 copy-start.1
Sparse Core Ops, SparseCore 0:
  10.7 44.5 all-gather.3
  57.1 50.8 all-gather.5
where the time goes:
time: 300 us; the launch traced here: 299 us
  waiting for transfers between devices  108 us (36%)
  blocking collectives  98.4 us (33%)
  Pallas kernels  53.1 us (18%)
  between operations  14.2 us (5%)
  starting transfers between devices  11.2 us (4%)
  local copies, waits for them, and re-layouts  9.59 us (3%)
    all_to_all x1, blocking collectives, shards(): lax.all_to_all(send_rows, 'exp', split_axis=0, concat_axis=0, tiled=True)  56.8 us
    all_to_all x1, waiting for transfers between devices, shards(): lax.all_to_all(processed, 'exp', split_axis=1, concat_axis=1, tiled=True)  48.9 us
    all_gather x1, waiting for transfers between devices, shards(): own_cols = lax.all_gather(own_cols, 'seq', axis=0, tiled=True)  46.4 us
    all_to_all x1, blocking collectives, shards(): lax.all_to_all(sent, 'seq', split_axis=0, concat_axis=0, tiled=True)  41.6 us
    pallas_call x1, Pallas kernels, expert(): pl.pallas_call(functools.partial(expert_kernel, up_steps), grid=(up_steps...  26.1 us
    pallas_call x1, Pallas kernels, attend(): pl.pallas_call(functools.partial(attend_kernel, blocks), grid=(sources //...  14 us
    all_to_all x1, waiting for transfers between devices, shards(): lax.all_to_all(attended, 'seq', split_axis=0, concat_axis=0, tiled=True)  13 us
    pallas_call x1, Pallas kernels, project(): pl.pallas_call(project_kernel, grid=(tiles,), out_shape=(jax.ShapeDtypeSt...  8.58 us
  transfers between devices with their start and end apart: 4, of which 3 were waited for; matrix products, arithmetic and copies ran while one was open for 1% of the time, Pallas kernels for 6%

commit v1 on v0

v1 whole, which is shorter than its diff:
```python
import functools
import math

import jax
import jax.numpy as jnp
from jax import lax
from jax.experimental import pallas as pl
from jax.experimental.pallas import tpu as pltpu
from jax.sharding import PartitionSpec as P

HEAD_DIM = 128
BF16 = jnp.bfloat16
F32 = jnp.float32
MIB = 2**20


def dot(a, b):
    return jnp.dot(a, b, preferred_element_type=F32)


def pack_kernel(*refs):
    ins, out = refs[:-1], refs[-1]
    heads = out.shape[0]
    for h in range(heads):
        for a, ref in enumerate(ins):
            out[h, a] = ref[:, h * HEAD_DIM : (h + 1) * HEAD_DIM]


def pack(arrays):
    rows, width = arrays[0].shape
    heads = width // HEAD_DIM
    step = 4
    return pl.pallas_call(
        pack_kernel,
        grid=(heads // step,),
        out_shape=jax.ShapeDtypeStruct((heads, len(arrays), rows, HEAD_DIM), BF16),
        in_specs=[pl.BlockSpec((rows, step * HEAD_DIM), lambda i: (0, i))] * len(arrays),
        out_specs=pl.BlockSpec((step, len(arrays), rows, HEAD_DIM), lambda i: (i, 0, 0, 0)),
        cost_estimate=pl.CostEstimate(
            flops=0, bytes_accessed=4 * len(arrays) * rows * width, transcendentals=0
        ),
        name="pack_heads",
    )(*arrays)


def attend_kernel(blocks, r_ref, o_ref, t_ref, kt, vv):
    sources, _, rows, _ = r_ref.shape
    i = pl.program_id(0)

    @pl.when(i == 0)
    def _():
        for s in range(sources):
            at = slice(s * rows, (s + 1) * rows)
            kt[:HEAD_DIM, at] = r_ref[s, 1].T
            kt[HEAD_DIM:, at] = r_ref[s, 4].T
            vv[at, :HEAD_DIM] = r_ref[s, 2]
            vv[at, HEAD_DIM:] = r_ref[s, 5]

    scale = 1.0 / math.sqrt(HEAD_DIM)
    q = r_ref[pl.ds(i * blocks, blocks), 0].reshape(blocks * rows, HEAD_DIM)
    dq = r_ref[pl.ds(i * blocks, blocks), 3].reshape(blocks * rows, HEAD_DIM)
    s = dot(q, kt[:HEAD_DIM])
    ds = dot(jnp.concatenate([dq, q], axis=1), kt[...])
    m = jnp.max(s, axis=-1, keepdims=True)
    e = jnp.exp2((s - m) * (scale * math.log2(math.e)))
    total = jnp.sum(e, axis=-1, keepdims=True)
    w = e * ds
    row_sum = jnp.sum(w, axis=-1, keepdims=True)
    both = dot(e.astype(BF16), vv[...])
    wv = dot(w.astype(BF16), vv[:, :HEAD_DIM])
    inv = 1.0 / total
    att = both[:, :HEAD_DIM] * inv
    tan = (wv * scale + both[:, HEAD_DIM:]) * inv - (row_sum * (inv * scale)) * att
    o_ref[...] = att.astype(BF16).reshape(blocks, rows, HEAD_DIM)
    t_ref[...] = tan.astype(BF16).reshape(blocks, rows, HEAD_DIM)


def attend(received, blocks=2):
    sources, _, rows, _ = received.shape
    seq_len = sources * rows
    shape = jax.ShapeDtypeStruct((sources, rows, HEAD_DIM), BF16)
    spec = pl.BlockSpec((blocks, rows, HEAD_DIM), lambda i: (i, 0, 0))
    return pl.pallas_call(
        functools.partial(attend_kernel, blocks),
        grid=(sources // blocks,),
        out_shape=(shape, shape),
        in_specs=[pl.BlockSpec(received.shape, lambda i: (0, 0, 0, 0))],
        out_specs=(spec, spec),
        scratch_shapes=[
            pltpu.VMEM((2 * HEAD_DIM, seq_len), BF16),
            pltpu.VMEM((seq_len, 2 * HEAD_DIM), BF16),
        ],
        compiler_params=pltpu.CompilerParams(vmem_limit_bytes=48 * MIB),
        cost_estimate=pl.CostEstimate(
            flops=16 * seq_len * seq_len * HEAD_DIM,
            bytes_accessed=16 * seq_len * HEAD_DIM,
            transcendentals=seq_len * seq_len,
        ),
        name="attend_head",
    )(received)


def accumulate(order, a_ref, w_refs, s_ref, acc, x):
    heads = a_ref.shape[0]
    for h in range(heads):
        x[:, h * HEAD_DIM : (h + 1) * HEAD_DIM] = a_ref[h]
    half = x.shape[1] // 2
    width = w_refs[0].shape[1]
    tile = 256
    for n in range(4):
        for c in range(0, width, tile):
            if n < 3:
                out = dot(x[...], w_refs[n][:, c : c + tile])
            else:
                out = dot(x[:, :half], w_refs[3][:half, c : c + tile]) + dot(
                    x[:, half:], w_refs[3][half:, c : c + tile]
                )
            at = pl.ds(pl.multiple_of(order[n] * width + c, tile), tile)
            acc[:, at] = out + s_ref[:, at].astype(F32)


def primal_kernel(order, a_ref, w0, w1, w2, w3, s_ref, g_ref, i_ref, h_ref, m_ref, x):
    accumulate(order, a_ref, (w0, w1, w2, w3), s_ref, h_ref, x)
    hid = h_ref[...]
    inverse = lax.rsqrt(jnp.mean(hid * hid, axis=-1, keepdims=True) + 1e-06)
    normed = (hid * inverse * g_ref[...].astype(F32)).astype(BF16)
    half = hid.shape[0] // 2
    info = i_ref.shape[0]
    m_ref[:half] = normed[:half]
    m_ref[half : half + info] = jnp.zeros((info, hid.shape[1]), BF16)
    m_ref[half : half + info, : i_ref.shape[1]] = i_ref[...]
    m_ref[half + info :] = normed[half:]


def tangent_kernel(order, a_ref, w0, w1, w2, w3, s_ref, g_ref, hid_ref, h_ref, m_ref, x):
    accumulate(order, a_ref, (w0, w1, w2, w3), s_ref, h_ref, x)
    hid = hid_ref[...]
    tan = h_ref[...]
    inverse = lax.rsqrt(jnp.mean(hid * hid, axis=-1, keepdims=True) + 1e-06)
    cross = jnp.mean(hid * tan, axis=-1, keepdims=True)
    m_ref[...] = (
        g_ref[...].astype(F32)
        * (tan * inverse - hid * (inverse * inverse * inverse) * cross)
    ).astype(BF16)


def project(kernel, order, attended, weights, stream, gain, extra, sent_rows):
    rows, width = stream.shape
    vmem = pl.BlockSpec(memory_space=pltpu.VMEM)
    return pl.pallas_call(
        kernel,
        out_shape=(
            jax.ShapeDtypeStruct((rows, width), F32),
            jax.ShapeDtypeStruct((sent_rows, width), BF16),
        ),
        in_specs=[pl.BlockSpec(memory_space=pltpu.SMEM)] + [vmem] * 8,
        out_specs=(vmem, vmem),
        scratch_shapes=[pltpu.VMEM((rows, width), BF16)],
        compiler_params=pltpu.CompilerParams(vmem_limit_bytes=48 * MIB),
        cost_estimate=pl.CostEstimate(
            flops=2 * rows * width * width, bytes_accessed=3 * width * width, transcendentals=0
        ),
        name="project_norm",
    )(order, attended, *weights, stream, gain, extra)


SLOTS = 64
INFO = 16
TILE = 128
COLS = 256


def expert_kernel(primal, rows, *refs):
    it = iter(refs)
    take = lambda n: [next(it) for _ in range(n)]
    (me,) = take(1)
    messages = take(8)
    gate, up, down = take(3)
    if primal:
        own, other, coef, disp, comb = take(5)
    else:
        coef_in, disp, comb = take(3)
        own, other = take(2)
    mb, wb, db, xs, hid, ct, msem, wsem, dsem = take(9)
    tokens, width = own.shape[1:]
    ff = gate.shape[1]
    x, s0, fp, fm, s1, f1, f2, s2 = messages
    cut = f1.shape[0]
    pieces = [
        (x, mb.at[0]),
        (s0, mb.at[1]),
        (fp, mb.at[2]),
        (s1.at[:rows], mb.at[3]),
        (fm, mb.at[4]),
        (s1.at[rows:], mb.at[5]),
        (f1, mb.at[6, :cut]),
        (f2, mb.at[6, cut:]),
        (s2, mb.at[7]),
    ]
    loads = [pltpu.make_async_copy(a, b, msem.at[n]) for n, (a, b) in enumerate(pieces)]
    for load in loads:
        load.start()

    def up_loads(f):
        at = pl.ds(pl.multiple_of(f * TILE, TILE), TILE)
        return (
            pltpu.make_async_copy(gate.at[:, at], wb.at[f, :, :TILE], wsem.at[0, f]),
            pltpu.make_async_copy(up.at[:, at], wb.at[f, :, TILE:], wsem.at[1, f]),
        )

    def down_load(j):
        at = pl.ds(pl.multiple_of(j * COLS, COLS), COLS)
        return pltpu.make_async_copy(down.at[:, at], db.at[j], dsem.at[j])

    for f in range(ff // TILE):
        for load in up_loads(f):
            load.start()
    for j in range(width // COLS):
        down_load(j).start()
    for load in loads:
        load.wait()

    for k in range(8):
        if primal:
            half = tokens // 2
            info = mb[k, half : half + INFO, :tokens].astype(F32)
            slot = lax.broadcasted_iota(jnp.int32, (SLOTS, tokens), 0).astype(F32)
            mine = me[0].astype(F32)
            d = jnp.zeros((SLOTS, tokens), F32)
            c = jnp.zeros((SLOTS, tokens), F32)
            for n in range(2):
                hit = (info[3 * n : 3 * n + 1] == mine) & (info[3 * n + 1 : 3 * n + 2] == slot)
                d = d + jnp.where(hit, 1.0, 0.0)
                c = c + jnp.where(hit, info[3 * n + 2 : 3 * n + 3], 0.0)
            disp[k] = d.astype(BF16)
            comb[k] = c.astype(BF16)
            ct[k] = c.T.astype(BF16)
            tok = jnp.concatenate([mb[k, :half], mb[k, half + INFO :]], axis=0)
        else:
            ct[k] = comb[k].astype(F32).T.astype(BF16)
            tok = mb[k]
        xs[k * SLOTS : (k + 1) * SLOTS] = dot(disp[k], tok).astype(BF16)

    def up_step(f, carry):
        for load in up_loads(f):
            load.wait()
        at = pl.ds(pl.multiple_of(f * TILE, TILE), TILE)
        both = dot(xs[...], wb[f])
        g, u = both[:, :TILE], both[:, TILE:]
        if primal:
            sig = jax.nn.sigmoid(g)
            act = g * sig
            hid[:, at] = (act * u).astype(BF16)
            coef[0, :, at] = (sig * (1.0 + g * (1.0 - sig)) * u).astype(BF16)
            coef[1, :, at] = act.astype(BF16)
        else:
            hid[:, at] = (
                coef_in[0, :, at].astype(F32) * g + coef_in[1, :, at].astype(F32) * u
            ).astype(BF16)
        return carry

    lax.fori_loop(0, ff // TILE, up_step, 0)

    def down_step(j, carry):
        down_load(j).wait()
        at = pl.ds(pl.multiple_of(j * COLS, COLS), COLS)
        out = dot(hid[...], db[j]).astype(BF16)
        for k in range(8):
            part = dot(ct[k], out[k * SLOTS : (k + 1) * SLOTS]).astype(BF16)
            (own, other)[k % 2][k // 2, :, at] = part
        return carry

    lax.fori_loop(0, width // COLS, down_step, 0)


def expert(primal, me, messages, weights, more):
    gate, up, down = weights
    width, ff = gate.shape
    tokens = more[1].shape[2] if more else messages[0].shape[0] - INFO
    rows = messages[0].shape[0]
    slots = 8 * SLOTS
    vmem = pl.BlockSpec(memory_space=pltpu.VMEM)
    anywhere = pl.BlockSpec(memory_space=pl.ANY)
    out_shape = [jax.ShapeDtypeStruct((4, tokens, width), BF16)] * 2
    if primal:
        out_shape += [
            jax.ShapeDtypeStruct((2, slots, ff), BF16),
            jax.ShapeDtypeStruct((8, SLOTS, tokens), BF16),
            jax.ShapeDtypeStruct((8, SLOTS, tokens), BF16),
        ]
    return pl.pallas_call(
        functools.partial(expert_kernel, primal, rows),
        out_shape=tuple(out_shape),
        in_specs=[pl.BlockSpec(memory_space=pltpu.SMEM)]
        + [anywhere] * 11
        + [vmem] * len(more),
        out_specs=(vmem,) * len(out_shape),
        scratch_shapes=[
            pltpu.VMEM((8, rows, width), BF16),
            pltpu.VMEM((ff // TILE, width, 2 * TILE), BF16),
            pltpu.VMEM((width // COLS, ff, COLS), BF16),
            pltpu.VMEM((slots, width), BF16),
            pltpu.VMEM((slots, ff), BF16),
            pltpu.VMEM((8, tokens, SLOTS), BF16),
            pltpu.SemaphoreType.DMA((9,)),
            pltpu.SemaphoreType.DMA((2, ff // TILE)),
            pltpu.SemaphoreType.DMA((width // COLS,)),
        ],
        compiler_params=pltpu.CompilerParams(vmem_limit_bytes=56 * MIB),
        cost_estimate=pl.CostEstimate(
            flops=6 * slots * width * ff,
            bytes_accessed=6 * width * ff + 24 * tokens * width,
            transcendentals=slots * ff,
        ),
        name="expert_primal" if primal else "expert_tangent",
    )(me, *messages, gate, up, down, *more)


def step_y(x, distance):
    chips = lax.axis_size("exp") // 2
    pairs = [
        (2 * y + c, 2 * ((y + distance) % chips) + c) for y in range(chips) for c in range(2)
    ]
    return lax.ppermute(x, "exp", pairs)


def swap(x):
    count = lax.axis_size("exp")
    return lax.ppermute(x, "exp", [(n, n ^ 1) for n in range(count)])


def gather_tokens(x, cut):
    s0 = swap(x)
    fp = step_y(x, 1)
    fm = step_y(x, -1)
    f1 = step_y(fp[:cut], 1)
    f2 = step_y(fm[cut:], -1)
    s1 = swap(jnp.concatenate([fp, fm], axis=0))
    s2 = swap(jnp.concatenate([f1, f2], axis=0))
    return [x, s0, fp, fm, s1, f1, f2, s2]


def reduce_tokens(base, own, other):
    got = swap(other)
    both = lambda n: own[n].astype(F32) + got[n].astype(F32)
    half = own.shape[1] // 2
    far = both(3).astype(BF16)
    r1 = step_y(far[:half], 1)
    r2 = step_y(far[half:], -1)
    after, before = both(2), both(1)
    ahead = jnp.concatenate([after[:half] + r1.astype(F32), after[half:]], axis=0).astype(BF16)
    back = jnp.concatenate([before[:half], before[half:] + r2.astype(F32)], axis=0).astype(BF16)
    r3 = step_y(ahead, 1)
    r4 = step_y(back, -1)
    mixed = both(0) + r3.astype(F32) + r4.astype(F32)
    return (base + mixed).astype(BF16)


def gather_projection(out_proj, own):
    y, core = own // 2, own % 2
    width = out_proj.shape[1]
    quarter = width // 4
    mine = (y % 2) * 2 + core
    part = lax.dynamic_slice_in_dim(out_proj, mine * quarter, quarter, axis=1)
    w0 = lax.all_gather(part, "seq", axis=0, tiled=True)
    half = w0.shape[0] // 2
    w1 = swap(w0)
    g1 = step_y(w0[:half], 1)
    g2 = step_y(w0[half:], -1)
    w2 = jnp.concatenate([g1, g2], axis=0)
    w3 = swap(w2)
    order = jnp.stack([mine, mine ^ 1, mine ^ 2, mine ^ 3]).astype(jnp.int32)
    return order, (w0, w1, w2, w3)


def shards(
    stream,
    stream_tangent,
    query_rows,
    key_rows,
    value_rows,
    query_tangent,
    key_tangent,
    value_tangent,
    out_proj,
    norm_gain,
    gate_weight,
    up_weight,
    down_weight,
    route_ids,
    route_weights,
):
    tok_dev = stream.shape[1]
    own = lax.axis_index("exp")
    order, weights = gather_projection(out_proj, own)

    sent = pack(
        [
            query_rows[0],
            key_rows[0],
            value_rows[0],
            query_tangent[0],
            key_tangent[0],
            value_tangent[0],
        ]
    )
    received = lax.all_to_all(sent, "seq", split_axis=0, concat_axis=0, tiled=True)
    attended, attended_tangent = attend(received)
    back = lax.all_to_all(attended, "seq", split_axis=0, concat_axis=0, tiled=True)
    back_tangent = lax.all_to_all(
        attended_tangent, "seq", split_axis=0, concat_axis=0, tiled=True
    )

    experts_total = lax.axis_size("exp")
    flat_ids = route_ids.reshape(-1)
    onehot = (flat_ids[:, None] == jnp.arange(experts_total, dtype=jnp.int32)[None, :]).astype(
        jnp.int32
    )
    rank_in = jnp.sum((jnp.cumsum(onehot, axis=0) - onehot) * onehot, axis=1)
    rank_in = rank_in.reshape(tok_dev, -1)
    ids = route_ids[0]
    fields = []
    for n in range(2):
        fields += [ids[:, n].astype(BF16), rank_in[:, n].astype(BF16), route_weights[0, :, n]]
    info = jnp.concatenate(
        [jnp.stack(fields), jnp.zeros((INFO - len(fields), tok_dev), BF16)], axis=0
    )

    gain = norm_gain.reshape(1, -1)
    hidden, message = project(
        primal_kernel, order, back, weights, stream[0], gain, info, tok_dev + INFO
    )
    hidden_tangent, message_tangent = project(
        tangent_kernel, order, back_tangent, weights, stream_tangent[0], gain, hidden, tok_dev
    )

    me = own.astype(jnp.int32).reshape(1)
    mats = (gate_weight[0], up_weight[0], down_weight[0])
    half = tok_dev // 2
    tokens = gather_tokens(message, half + INFO)
    tokens_tangent = gather_tokens(message_tangent, half)
    part, part_other, *more = expert(True, me, tokens, mats, [])
    dpart, dpart_other = expert(False, me, tokens_tangent, mats, more)
    layer_out = reduce_tokens(hidden, part, part_other)
    layer_tangent = reduce_tokens(hidden_tangent, dpart, dpart_other)
    return (layer_out[None], layer_tangent[None])


def solution(mesh):
    rows = P("exp", "seq", None)
    in_specs = (rows,) * 8 + (
        P("seq", None),
        P(),
        P("exp", None, None),
        P("exp", None, None),
        P("exp", None, None),
        rows,
        rows,
    )
    return jax.shard_map(
        shards, mesh=mesh, in_specs=in_specs, out_specs=(rows, rows), check_vma=False
    )
```

time: 300 us -> 327 us (1.090)
  blocking collectives: 98.4 us -> 0 us
  starting transfers between devices: 11.2 us -> 56.4 us
  waiting for transfers between devices: 108 us -> 143 us
  Pallas kernels: 53.1 us -> 85.3 us
  local copies, waits for them, and re-layouts: 9.59 us -> 17.4 us
  other arithmetic: 2.11 us -> 8 us
    all_to_all x2 -> x0, blocking collectives: 98.4 us -> none  [the longest x1 56.8 us: shards(): lax.all_to_all(send_rows, 'exp', split_axis=0, concat_axis=0, tiled=True)]
    ppermute x0 -> x28, waiting for transfers between devices: none -> 64.1 us  [the longest x18 62 us: step_y(): return lax.ppermute(x, 'exp', pairs)]
    all_to_all x1 -> x2, waiting for transfers between devices: 48.9 us -> 4.57 us  [the longest x1 4.57 us: shards(): lax.all_to_all(attended_tangent, 'seq', split_axis=0, concat_axis=0, tile...]
    ppermute x0 -> x28, starting transfers between devices: none -> 38.9 us  [the longest x18 22.5 us: step_y(): return lax.ppermute(x, 'exp', pairs)]
    pallas_call x2 -> x4, Pallas kernels: 34.7 us -> 64.9 us  [the longest x2 55.1 us: expert(): pl.pallas_call(functools.partial(expert_kernel, primal, rows), out_shape=...]
    all_gather x2 -> x1, waiting for transfers between devices: 46.4 us -> 65.4 us  [gather_projection(): w0 = lax.all_gather(part, 'seq', axis=0, tiled=True)]
    all_to_all x1 -> x2, starting transfers between devices: 5.58 us -> 12.8 us  [the longest x1 8.47 us: shards(): lax.all_to_all(sent, 'seq', split_axis=0, concat_axis=0, tiled=True)]
    unnamed x15 -> x52, local copies, waits for them, and re-layouts: 3.21 us -> 8.64 us
  transfers between devices with their start and end apart: 4 -> 32, of which waited for: 3 -> 16; matrix products, arithmetic and copies ran while one was open for 1% -> 5% of each run, Pallas kernels for 6% -> 25%
where the time goes in v1:
time: 327 us; the launch traced here: 325 us
  waiting for transfers between devices  143 us (44%)
  Pallas kernels  85.3 us (26%)
  starting transfers between devices  56.4 us (17%)
  local copies, waits for them, and re-layouts  17.4 us (5%)
  between operations  14.5 us (4%)
  other arithmetic  8 us (2%)
    all_gather x1, waiting for transfers between devices, gather_projection(): w0 = lax.all_gather(part, 'seq', axis=0, tiled=True)  65.4 us
    ppermute x18, waiting for transfers between devices, step_y(): return lax.ppermute(x, 'exp', pairs)  62 us
    pallas_call x2, Pallas kernels, expert(): pl.pallas_call(functools.partial(expert_kernel, primal, rows), out_shape=...  55.1 us
    ppermute x18, starting transfers between devices, step_y(): return lax.ppermute(x, 'exp', pairs)  22.5 us
    ppermute x10, starting transfers between devices, swap(): return lax.ppermute(x, 'exp', [(n, n ^ 1) for n in range(count)])  16.4 us
    pallas_call x1, Pallas kernels, attend(): pl.pallas_call(functools.partial(attend_kernel, blocks), grid=(sources //...  15.9 us
    pallas_call x2, Pallas kernels, project(): pl.pallas_call(kernel, out_shape=(jax.ShapeDtypeStruct((rows, width), F32...  9.78 us
    all_to_all x1, waiting for transfers between devices, shards(): lax.all_to_all(attended, 'seq', split_axis=0, concat_axis=0, tiled=True)  9.4 us
  transfers between devices with their start and end apart: 32, of which 16 were waited for; matrix products, arithmetic and copies ran while one was open for 5% of the time, Pallas kernels for 25%

profile of v1, /device:TPU:1, one launch (start us, length us, event | category | flops | bytes accessed | tf_op | source)
XLA Modules:
  0.0 325.1 jit_solution(6041332156990906348)
XLA Ops:
  8.9 4.4 %pack_heads.1 = bf16[16,6,128,128]{3,2,1,0:T(8,128)(2,1)} custom-call(bf16[128,2048]{1,0:T(8,128)(2,1)} %bitcast.102, bf16[128,2048]{1,0:T(8,128)(2,1)} %bitcast.103, bf16[128,2048]{1,0:T(8,128)(2,1)} %bitcast.104, bf16[128,2048]{1,0:T(8,128)(2,1)} %bitcast.105, bf16[128,2048]{1,0:T(8,128)(2,1)} %bitcast.106, bf16[128,2048]{1,0:T(8,128)(2,1)} %bitcast.107), custom_call_target="tpu_custom_call" | custom-call | bytes 6291456 | tf_op jit(solution)/shard_map/pack_heads/pallas_call | solution.py:33
  13.3 8.5 %all-to-all-start = ((bf16[16,6,128,128]{3,2,1,0:T(8,128)(2,1)}), bf16[16,6,128,128]{3,2,1,0:T(8,128)(2,1)}, u32[]{:S(2)}, u32[]{:S(2)}) async-start(bf16[16,6,128,128]{3,2,1,0:T(8,128)(2,1)} %pack_heads.1), calls=%async_computation | async-start | bytes 6291456 | tf_op jit(solution)/shard_map/all_to_all | solution.py:407
  21.8 65.4 %all-gather.2.cloned.1.call-done.w0 = bf16[2048,512]{1,0:T(8,128)(2,1)} async-done(((bf16[128,512]{1,0:T(8,128)(2,1)}), bf16[2048,512]{1,0:T(8,128)(2,1)}) %all-gather.2.cloned.1.call-update) | async-done | bytes 2097168 | tf_op jit(solution)/shard_map/all_gather | solution.py:365
  87.2 3.2 fusion.23
  95.8 19.0 %collective-permute-done.1 = bf16[1024,512]{1,0:T(8,128)(2,1)} collective-permute-done((bf16[1024,512]{1,0:T(8,128)(2,1)}, bf16[1024,512]{1,0:T(8,128)(2,1)}, u32[]{:S(2)}, u32[]{:S(2)}) %collective-permute-start.1) | collective-permute-done | bytes 1048608 | tf_op jit(solution)/shard_map/ppermute | solution.py:324
  122.9 15.9 %attend_head.1 = (bf16[16,128,128]{2,1,0:T(8,128)(2,1)}, bf16[16,128,128]{2,1,0:T(8,128)(2,1)S(1)}) custom-call(bf16[16,6,128,128]{3,2,1,0:T(8,128)(2,1)} %all-to-all-done.r_ref), custom_call_target="tpu_custom_call" | custom-call | flops 8589934592 | bytes 4194304 | tf_op jit(solution)/shard_map/attend_head/pallas_call | solution.py:83
  139.6 4.7 %all-to-all-start.1 = ((bf16[16,128,128]{2,1,0:T(8,128)(2,1)}), bf16[16,128,128]{2,1,0:T(8,128)(2,1)S(1)}, u32[]{:S(2)}, u32[]{:S(2)}) async-start(bf16[16,128,128]{2,1,0:T(8,128)(2,1)} %get-tuple-element.15), calls=%async_computation.1 | async-start | bytes 1048576 | tf_op jit(solution)/shard_map/all_to_all | solution.py:409
  145.0 9.4 %all-to-all-done.1.a_ref = bf16[16,128,128]{2,1,0:T(8,128)(2,1)S(1)} async-done(((bf16[16,128,128]{2,1,0:T(8,128)(2,1)}), bf16[16,128,128]{2,1,0:T(8,128)(2,1)S(1)}, u32[]{:S(2)}, u32[]{:S(2)}) %all-to-all-start.1) | async-done | bytes 524320 | tf_op jit(solution)/shard_map/all_to_all | solution.py:409
  155.5 5.3 %project_norm.2 = (f32[128,2048]{1,0:T(8,128)S(1)}, bf16[144,2048]{1,0:T(8,128)(2,1)}) custom-call(s32[4]{0:T(128)S(1)} %pad_add_fusion.order, bf16[16,128,128]{2,1,0:T(8,128)(2,1)S(1)} %all-to-all-done.1.a_ref, bf16[2048,512]{1,0:T(8,128)(2,1)S(1)} %copy-done.2, bf16[2048,512]{1,0:T(8,128)(2,1)} %collective-permute-done.w1, ...), custom_call_target="tpu_custom_call" | custom-call | flops 1073741824 | bytes 12582912 | tf_op jit(solution)/shard_map/project_norm/pallas_call | solution.py:150
  163.3 11.3 %collective-permute-done.6.refs_4_ = bf16[144,2048]{1,0:T(8,128)(2,1)S(1)} collective-permute-done((bf16[144,2048]{1,0:T(8,128)(2,1)}, bf16[144,2048]{1,0:T(8,128)(2,1)S(1)}, u32[]{:S(2)}, u32[]{:S(2)}) %collective-permute-start.6) | collective-permute-done | bytes 589856 | tf_op jit(solution)/shard_map/ppermute | solution.py:324
  177.9 3.5 %collective-permute-start.7 = (bf16[288,2048]{1,0:T(8,128)(2,1)}, bf16[288,2048]{1,0:T(8,128)(2,1)}, u32[]{:S(2)}, u32[]{:S(2)}) collective-permute-start(bf16[288,2048]{1,0:T(8,128)(2,1)} %pad_maximum_fusion), channel_id=1, source_target_pairs={{0,1},{1,0},{2,3},{3,2},{4,5},{5,4},{6,7},{7,6},{8,9},{9,8},{10,11... | collective-permute-start | bytes 3538952 | tf_op jit(solution)/shard_map/ppermute | solution.py:329
  182.9 2.7 collective-permute-start.9
  185.5 4.4 %all-to-all-start.2 = ((bf16[16,128,128]{2,1,0:T(8,128)(2,1)}), bf16[16,128,128]{2,1,0:T(8,128)(2,1)S(1)}, u32[]{:S(2)}, u32[]{:S(2)}) async-start(bf16[16,128,128]{2,1,0:T(8,128)(2,1)} %copy-done.8), calls=%async_computation.2 | async-start | bytes 1048576 | tf_op jit(solution)/shard_map/all_to_all | solution.py:410
  195.6 4.6 %all-to-all-done.2.a_ref = bf16[16,128,128]{2,1,0:T(8,128)(2,1)S(1)} async-done(((bf16[16,128,128]{2,1,0:T(8,128)(2,1)}), bf16[16,128,128]{2,1,0:T(8,128)(2,1)S(1)}, u32[]{:S(2)}, u32[]{:S(2)}) %all-to-all-start.2) | async-done | bytes 524320 | tf_op jit(solution)/shard_map/all_to_all | solution.py:410
  201.4 4.5 %project_norm.3 = (f32[128,2048]{1,0:T(8,128)S(1)}, bf16[128,2048]{1,0:T(8,128)(2,1)S(1)}) custom-call(s32[4]{0:T(128)S(1)} %pad_add_fusion.order, bf16[16,128,128]{2,1,0:T(8,128)(2,1)S(1)} %all-to-all-done.2.a_ref, bf16[2048,512]{1,0:T(8,128)(2,1)S(1)} %copy-done.2, bf16[2048,512]{1,0:T(8,128)(2,1)} %collective-permute-done.w1, ...), custom_call_target="tpu_custom_call" | custom-call | flops 1073741824 | bytes 12582912 | tf_op jit(solution)/shard_map/project_norm/pallas_call | solution.py:150
  207.5 27.2 %expert_primal.1 = (bf16[4,128,2048]{2,1,0:T(8,128)(2,1)}, bf16[4,128,2048]{2,1,0:T(8,128)(2,1)}, bf16[2,512,1408]{2,1,0:T(8,128)(2,1)}, bf16[8,64,128]{2,1,0:T(8,128)(2,1)}, bf16[8,64,128]{2,1,0:T(8,128)(2,1)}) custom-call(s32[1]{0:T(128)} %bitcast.18.refs_0_, bf16[144,2048]{1,0:T(8,128)(2,1)} %get-tuple-element.17.refs_1_, ...), custom_call_target="tpu_custom_call" | custom-call | flops 8858370048 | bytes 23592960 | tf_op jit(solution)/shard_map/expert_primal/pallas_call | solution.py:291
  234.7 2.8 collective-permute-start.11
  240.4 4.8 %collective-permute-done.21.refs_7_ = bf16[64,2048]{1,0:T(8,128)(2,1)S(1)} collective-permute-done((bf16[64,2048]{1,0:T(8,128)(2,1)S(1)}, bf16[64,2048]{1,0:T(8,128)(2,1)S(1)}, u32[]{:S(2)}, u32[]{:S(2)}) %collective-permute-start.21) | collective-permute-done | bytes 262176 | tf_op jit(solution)/shard_map/ppermute | solution.py:324
  251.9 28.0 %expert_tangent.1 = (bf16[4,128,2048]{2,1,0:T(8,128)(2,1)}, bf16[4,128,2048]{2,1,0:T(8,128)(2,1)}) custom-call(s32[1]{0:T(128)} %bitcast.18.refs_0_, bf16[128,2048]{1,0:T(8,128)(2,1)} %copy-done.9, bf16[128,2048]{1,0:T(8,128)(2,1)} %copy-done.23, bf16[128,2048]{1,0:T(8,128)(2,1)} %copy-done.15, bf16[128,2048]{1,0:T(8,128)(2,1)} %copy-done.14, ...), custom_call_target="tpu_custom_call" | custom-call | flops 8858370048 | bytes 23592960 | tf_op jit(solution)/shard_map/expert_tangent/pallas_call | solution.py:291
  285.1 2.7 collective-permute-start.26
  289.1 3.5 %collective-permute-start.15 = (bf16[128,2048]{1,0:T(8,128)(2,1)S(1)}, bf16[128,2048]{1,0:T(8,128)(2,1)S(1)}, u32[]{:S(2)}, u32[]{:S(2)}) collective-permute-start(bf16[128,2048]{1,0:T(8,128)(2,1)S(1)} %pad_maximum_fusion.4), channel_id=1, source_target_pairs={{0,6},{1,7},{2,0},{3,1},{4,2},{5,3},{6,4},{7,5},{8,14},{9,15},{10,... | collective-permute-start | bytes 1572872 | tf_op jit(solution)/shard_map/ppermute | solution.py:324
  294.7 3.5 %collective-permute-start.27 = (bf16[128,2048]{1,0:T(8,128)(2,1)S(1)}, bf16[128,2048]{1,0:T(8,128)(2,1)S(1)}, u32[]{:S(2)}, u32[]{:S(2)}) collective-permute-start(bf16[128,2048]{1,0:T(8,128)(2,1)S(1)} %pad_maximum_fusion.7), channel_id=1, source_target_pairs={{0,6},{1,7},{2,0},{3,1},{4,2},{5,3},{6,4},{7,5},{8,14},{9,15},{10,... | collective-permute-start | bytes 1572872 | tf_op jit(solution)/shard_map/ppermute | solution.py:324
  298.4 7.4 %collective-permute-done.15 = bf16[128,2048]{1,0:T(8,128)(2,1)S(1)} collective-permute-done((bf16[128,2048]{1,0:T(8,128)(2,1)S(1)}, bf16[128,2048]{1,0:T(8,128)(2,1)S(1)}, u32[]{:S(2)}, u32[]{:S(2)}) %collective-permute-start.15) | collective-permute-done | bytes 524320 | tf_op jit(solution)/shard_map/ppermute | solution.py:324
  307.0 10.0 %collective-permute-done.27 = bf16[128,2048]{1,0:T(8,128)(2,1)S(1)} collective-permute-done((bf16[128,2048]{1,0:T(8,128)(2,1)S(1)}, bf16[128,2048]{1,0:T(8,128)(2,1)S(1)}, u32[]{:S(2)}, u32[]{:S(2)}) %collective-permute-start.27) | collective-permute-done | bytes 524320 | tf_op jit(solution)/shard_map/ppermute | solution.py:324
  (146 shorter events, 54.2 us)
Async XLA Ops:
  7.2 80.0 %all-gather.2.cloned.1.call-start = ((), (), s32[]{:S(2)}) async-start(), calls=%async_computation.3 | async-start | bytes 2228224 | tf_op jit(solution)/shard_map/all_gather | solution.py:365
  13.3 109.6 %all-to-all-start = ((bf16[16,6,128,128]{3,2,1,0:T(8,128)(2,1)}), bf16[16,6,128,128]{3,2,1,0:T(8,128)(2,1)}, u32[]{:S(2)}, u32[]{:S(2)}) async-start(bf16[16,6,128,128]{3,2,1,0:T(8,128)(2,1)} %pack_heads.1), calls=%async_computation | async-start | bytes 6291456 | tf_op jit(solution)/shard_map/all_to_all | solution.py:407
  90.4 24.4 %collective-permute-start.1 = (bf16[1024,512]{1,0:T(8,128)(2,1)}, bf16[1024,512]{1,0:T(8,128)(2,1)}, u32[]{:S(2)}, u32[]{:S(2)}) collective-permute-start(bf16[1024,512]{1,0:T(8,128)(2,1)} %get-tuple-element.37), channel_id=1, source_target_pairs={{0,2},{1,3},{2,4},{3,5},{4,6},{5,7},{6,0},{7,1},{8,10},{9,11},{10,... | collective-permute-start | bytes 3145736 | tf_op jit(solution)/shard_map/ppermute | solution.py:324
  91.6 25.5 %collective-permute-start.2 = (bf16[1024,512]{1,0:T(8,128)(2,1)}, bf16[1024,512]{1,0:T(8,128)(2,1)}, u32[]{:S(2)}, u32[]{:S(2)}) collective-permute-start(bf16[1024,512]{1,0:T(8,128)(2,1)} %get-tuple-element.36), channel_id=1, source_target_pairs={{0,6},{1,7},{2,0},{3,1},{4,2},{5,3},{6,4},{7,5},{8,14},{9,15},{10,... | collective-permute-start | bytes 3145736 | tf_op jit(solution)/shard_map/ppermute | solution.py:324
  93.5 61.0 %collective-permute-start = (bf16[2048,512]{1,0:T(8,128)(2,1)S(1)}, bf16[2048,512]{1,0:T(8,128)(2,1)}, u32[]{:S(2)}, u32[]{:S(2)}) collective-permute-start(bf16[2048,512]{1,0:T(8,128)(2,1)S(1)} %copy-done.2), channel_id=1, source_target_pairs={{0,1},{1,0},{2,3},{3,2},{4,5},{5,4},{6,7},{7,6},{8,9},{9,8},{10,11... | collective-permute-start | bytes 6291464 | tf_op jit(solution)/shard_map/ppermute | solution.py:329
  119.4 35.1 %collective-permute-start.3 = (bf16[2048,512]{1,0:T(8,128)(2,1)}, bf16[2048,512]{1,0:T(8,128)(2,1)}, u32[]{:S(2)}, u32[]{:S(2)}) collective-permute-start(bf16[2048,512]{1,0:T(8,128)(2,1)} %constant_dynamic-update-slice_fusion.w2), channel_id=1, source_target_pairs={{0,1},{1,0},{2,3},{3,2},{4,5},{5,4},{6,7},{7,6},{8,9},{9,8},{10,11... | collective-permute-start | bytes 6291464 | tf_op jit(solution)/shard_map/ppermute | solution.py:329
  139.6 14.8 %all-to-all-start.1 = ((bf16[16,128,128]{2,1,0:T(8,128)(2,1)}), bf16[16,128,128]{2,1,0:T(8,128)(2,1)S(1)}, u32[]{:S(2)}, u32[]{:S(2)}) async-start(bf16[16,128,128]{2,1,0:T(8,128)(2,1)} %get-tuple-element.15), calls=%async_computation.1 | async-start | bytes 1048576 | tf_op jit(solution)/shard_map/all_to_all | solution.py:409
  161.8 12.7 %collective-permute-start.6 = (bf16[144,2048]{1,0:T(8,128)(2,1)}, bf16[144,2048]{1,0:T(8,128)(2,1)S(1)}, u32[]{:S(2)}, u32[]{:S(2)}) collective-permute-start(bf16[144,2048]{1,0:T(8,128)(2,1)} %get-tuple-element.17.refs_1_), channel_id=1, source_target_pairs={{0,6},{1,7},{2,0},{3,1},{4,2},{5,3},{6,4},{7,5},{8,14},{9,15},{10,... | collective-permute-start | bytes 1769480 | tf_op jit(solution)/shard_map/ppermute | solution.py:324
  163.0 13.7 %collective-permute-start.5 = (bf16[144,2048]{1,0:T(8,128)(2,1)}, bf16[144,2048]{1,0:T(8,128)(2,1)S(1)}, u32[]{:S(2)}, u32[]{:S(2)}) collective-permute-start(bf16[144,2048]{1,0:T(8,128)(2,1)} %get-tuple-element.17.refs_1_), channel_id=1, source_target_pairs={{0,2},{1,3},{2,4},{3,5},{4,6},{5,7},{6,0},{7,1},{8,10},{9,11},{10,... | collective-permute-start | bytes 1769480 | tf_op jit(solution)/shard_map/ppermute | solution.py:324
  177.9 29.6 %collective-permute-start.7 = (bf16[288,2048]{1,0:T(8,128)(2,1)}, bf16[288,2048]{1,0:T(8,128)(2,1)}, u32[]{:S(2)}, u32[]{:S(2)}) collective-permute-start(bf16[288,2048]{1,0:T(8,128)(2,1)} %pad_maximum_fusion), channel_id=1, source_target_pairs={{0,1},{1,0},{2,3},{3,2},{4,5},{5,4},{6,7},{7,6},{8,9},{9,8},{10,11... | collective-permute-start | bytes 3538952 | tf_op jit(solution)/shard_map/ppermute | solution.py:329
  182.2 10.8 %collective-permute-start.8 = (bf16[80,2048]{1,0:T(8,128)(2,1)}, bf16[80,2048]{1,0:T(8,128)(2,1)S(1)}, u32[]{:S(2)}, u32[]{:S(2)}) collective-permute-start(bf16[80,2048]{1,0:T(8,128)(2,1)} %slice.229), channel_id=1, source_target_pairs={{0,2},{1,3},{2,4},{3,5},{4,6},{5,7},{6,0},{7,1},{8,10},{9,11},{10,... | collective-permute-start | bytes 983048 | tf_op jit(solution)/shard_map/ppermute | solution.py:324
  185.5 14.7 %all-to-all-start.2 = ((bf16[16,128,128]{2,1,0:T(8,128)(2,1)}), bf16[16,128,128]{2,1,0:T(8,128)(2,1)S(1)}, u32[]{:S(2)}, u32[]{:S(2)}) async-start(bf16[16,128,128]{2,1,0:T(8,128)(2,1)} %copy-done.8), calls=%async_computation.2 | async-start | bytes 1048576 | tf_op jit(solution)/shard_map/all_to_all | solution.py:410
  189.9 17.6 %collective-permute-start.4 = (bf16[144,2048]{1,0:T(8,128)(2,1)}, bf16[144,2048]{1,0:T(8,128)(2,1)}, u32[]{:S(2)}, u32[]{:S(2)}) collective-permute-start(bf16[144,2048]{1,0:T(8,128)(2,1)} %get-tuple-element.17.refs_1_), channel_id=1, source_target_pairs={{0,1},{1,0},{2,3},{3,2},{4,5},{5,4},{6,7},{7,6},{8,9},{9,8},{10,11... | collective-permute-start | bytes 1769480 | tf_op jit(solution)/shard_map/ppermute | solution.py:329
  194.8 12.7 %collective-permute-start.10 = (bf16[144,2048]{1,0:T(8,128)(2,1)}, bf16[144,2048]{1,0:T(8,128)(2,1)}, u32[]{:S(2)}, u32[]{:S(2)}) collective-permute-start(bf16[144,2048]{1,0:T(8,128)(2,1)} %pad_maximum_fusion.2), channel_id=1, source_target_pairs={{0,1},{1,0},{2,3},{3,2},{4,5},{5,4},{6,7},{7,6},{8,9},{9,8},{10,11... | collective-permute-start | bytes 1769480 | tf_op jit(solution)/shard_map/ppermute | solution.py:329
  206.0 31.5 %collective-permute-start.18 = (bf16[128,2048]{1,0:T(8,128)(2,1)S(1)}, bf16[128,2048]{1,0:T(8,128)(2,1)S(1)}, u32[]{:S(2)}, u32[]{:S(2)}) collective-permute-start(bf16[128,2048]{1,0:T(8,128)(2,1)S(1)} %get-tuple-element.22.refs_1_), channel_id=1, source_target_pairs={{0,6},{1,7},{2,0},{3,1},{4,2},{5,3},{6,4},{7,5},{8,14},{9,15},{10,... | collective-permute-start | bytes 1572872 | tf_op jit(solution)/shard_map/ppermute | solution.py:324
  206.1 31.4 %collective-permute-start.17 = (bf16[128,2048]{1,0:T(8,128)(2,1)S(1)}, bf16[128,2048]{1,0:T(8,128)(2,1)S(1)}, u32[]{:S(2)}, u32[]{:S(2)}) collective-permute-start(bf16[128,2048]{1,0:T(8,128)(2,1)S(1)} %get-tuple-element.22.refs_1_), channel_id=1, source_target_pairs={{0,2},{1,3},{2,4},{3,5},{4,6},{5,7},{6,0},{7,1},{8,10},{9,11},{10,... | collective-permute-start | bytes 1572872 | tf_op jit(solution)/shard_map/ppermute | solution.py:324
  234.7 45.6 %collective-permute-start.11 = (bf16[4,128,2048]{2,1,0:T(8,128)(2,1)}, bf16[4,128,2048]{2,1,0:T(8,128)(2,1)S(1)}, u32[]{:S(2)}, u32[]{:S(2)}) collective-permute-start(bf16[4,128,2048]{2,1,0:T(8,128)(2,1)} %get-tuple-element.19), channel_id=1, source_target_pairs={{0,1},{1,0},{2,3},{3,2},{4,5},{5,4},{6,7},{7,6},{8,9},{9,8},{10,11... | collective-permute-start | bytes 6291464 | tf_op jit(solution)/shard_map/ppermute | solution.py:329
  237.6 13.1 %collective-permute-start.19 = (bf16[256,2048]{1,0:T(8,128)(2,1)S(1)}, bf16[256,2048]{1,0:T(8,128)(2,1)S(1)}, u32[]{:S(2)}, u32[]{:S(2)}) collective-permute-start(bf16[256,2048]{1,0:T(8,128)(2,1)S(1)} %pad_maximum_fusion.1), channel_id=1, source_target_pairs={{0,1},{1,0},{2,3},{3,2},{4,5},{5,4},{6,7},{7,6},{8,9},{9,8},{10,11... | collective-permute-start | bytes 3145736 | tf_op jit(solution)/shard_map/ppermute | solution.py:329
  281.0 11.6 %collective-permute-start.12 = (bf16[64,2048]{1,0:T(8,128)(2,1)S(1)}, bf16[64,2048]{1,0:T(8,128)(2,1)S(1)}, u32[]{:S(2)}, u32[]{:S(2)}) collective-permute-start(bf16[64,2048]{1,0:T(8,128)(2,1)S(1)} %get-tuple-element.40), channel_id=1, source_target_pairs={{0,2},{1,3},{2,4},{3,5},{4,6},{5,7},{6,0},{7,1},{8,10},{9,11},{10,... | collective-permute-start | bytes 786440 | tf_op jit(solution)/shard_map/ppermute | solution.py:324
  285.0 13.2 %collective-permute-start.24 = (bf16[64,2048]{1,0:T(8,128)(2,1)S(1)}, bf16[64,2048]{1,0:T(8,128)(2,1)S(1)}, u32[]{:S(2)}, u32[]{:S(2)}) collective-permute-start(bf16[64,2048]{1,0:T(8,128)(2,1)S(1)} %get-tuple-element.38), channel_id=1, source_target_pairs={{0,2},{1,3},{2,4},{3,5},{4,6},{5,7},{6,0},{7,1},{8,10},{9,11},{10,... | collective-permute-start | bytes 786440 | tf_op jit(solution)/shard_map/ppermute | solution.py:324
  289.1 16.8 %collective-permute-start.15 = (bf16[128,2048]{1,0:T(8,128)(2,1)S(1)}, bf16[128,2048]{1,0:T(8,128)(2,1)S(1)}, u32[]{:S(2)}, u32[]{:S(2)}) collective-permute-start(bf16[128,2048]{1,0:T(8,128)(2,1)S(1)} %pad_maximum_fusion.4), channel_id=1, source_target_pairs={{0,6},{1,7},{2,0},{3,1},{4,2},{5,3},{6,4},{7,5},{8,14},{9,15},{10,... | collective-permute-start | bytes 1572872 | tf_op jit(solution)/shard_map/ppermute | solution.py:324
  292.6 13.2 %collective-permute-start.13 = (bf16[128,2048]{1,0:T(8,128)(2,1)S(1)}, bf16[128,2048]{1,0:T(8,128)(2,1)S(1)}, u32[]{:S(2)}, u32[]{:S(2)}) collective-permute-start(bf16[128,2048]{1,0:T(8,128)(2,1)S(1)} %pad_maximum_fusion.3), channel_id=1, source_target_pairs={{0,2},{1,3},{2,4},{3,5},{4,6},{5,7},{6,0},{7,1},{8,10},{9,11},{10,... | collective-permute-start | bytes 1572872 | tf_op jit(solution)/shard_map/ppermute | solution.py:324
  294.7 22.4 %collective-permute-start.27 = (bf16[128,2048]{1,0:T(8,128)(2,1)S(1)}, bf16[128,2048]{1,0:T(8,128)(2,1)S(1)}, u32[]{:S(2)}, u32[]{:S(2)}) collective-permute-start(bf16[128,2048]{1,0:T(8,128)(2,1)S(1)} %pad_maximum_fusion.7), channel_id=1, source_target_pairs={{0,6},{1,7},{2,0},{3,1},{4,2},{5,3},{6,4},{7,5},{8,14},{9,15},{10,... | collective-permute-start | bytes 1572872 | tf_op jit(solution)/shard_map/ppermute | solution.py:324
  298.3 18.8 %collective-permute-start.25 = (bf16[128,2048]{1,0:T(8,128)(2,1)S(1)}, bf16[128,2048]{1,0:T(8,128)(2,1)S(1)}, u32[]{:S(2)}, u32[]{:S(2)}) collective-permute-start(bf16[128,2048]{1,0:T(8,128)(2,1)S(1)} %pad_maximum_fusion.6), channel_id=1, source_target_pairs={{0,2},{1,3},{2,4},{3,5},{4,6},{5,7},{6,0},{7,1},{8,10},{9,11},{10,... | collective-permute-start | bytes 1572872 | tf_op jit(solution)/shard_map/ppermute | solution.py:324
  (33 other events, 357.8 us)
Sparse Core Ops, SparseCore 0:
  10.7 76.4 all-gather.1
